TPU v7x, 128 devices: a whole 4x4x4 slice. The times are simulated.
128 devices in a mesh: tm: 8 (over y_lo, z), space: 16 (over y_hi, x, core).
Axes of the slice: x: 4, y: 4 (y_hi: 2, y_lo: 2; y = y_hi * 2 + y_lo), z: 4, core: 2. Of those that a mesh axis runs over, the one named last changes fastest.
Arguments:
- snapshots: bfloat16 [1024, 786432], P('tm', 'space'), may hold values from -10 to 10, as said below
- area_weight: float32 [786432], P('space'), may hold values from 0.1 to 1
- eigvecs: bfloat16 [1024, 64], replicated, may hold values from -0.1875 to 0.1875
- eigvals: float32 [64], replicated, may hold values from 0.5 to 8
Outputs:
- gram: float32 [1024, 1024], P(('tm', 'space'))
- modes: bfloat16 [64, 786432], P('tm', 'space')
Inputs may be any that keep to these rules, and one draw needn't show every extreme that they name: `snapshots`: a per-column climatology plus hourly departures.
All inputs are finite; a program needn't handle non-finite values.
Results may differ from a plain program's by a relative error of at most 0.01.
Values may be sent and summed in bfloat16 or wider, within the bound.
A program may use at most 128 MiB of HBM per device.

v0:
```python
import jax
import jax.numpy as jnp
from jax import lax
from jax.sharding import PartitionSpec as P


def gram_local(weighted):
    return lax.dot_general(
        weighted, weighted, (((1,), (1,)), ((), ())), preferred_element_type=jnp.float32
    )


def local(snapshots, area_weight, eigvecs, eigvals):
    tm_count = lax.axis_size("tm")
    space_count = lax.axis_size("space")
    time_dev, cell_dev = snapshots.shape
    times = time_dev * tm_count
    cells = cell_dev * space_count
    sub_cells = cell_dev // tm_count
    mode_count = eigvecs.shape[1]
    mode_dev = mode_count // tm_count
    tm_index = lax.axis_index("tm")
    columns = lax.all_to_all(snapshots, "tm", split_axis=1, concat_axis=0, tiled=True)
    mean = jnp.sum(columns.astype(jnp.float32), axis=0) / times
    root = jnp.sqrt(area_weight)
    own_root = lax.dynamic_slice_in_dim(root, tm_index * sub_cells, sub_cells, 0)
    weighted = (own_root[None, :] * (columns.astype(jnp.float32) - mean[None, :])).astype(
        jnp.bfloat16
    )
    partial_gram = gram_local(weighted) / cells
    row_sums = lax.psum_scatter(
        partial_gram.astype(jnp.bfloat16), "tm", scatter_dimension=0, tiled=True
    )
    gram = lax.psum_scatter(row_sums, "space", scatter_dimension=0, tiled=True).astype(jnp.float32)
    inv_root = 1.0 / jnp.sqrt(eigvals)
    all_means = lax.all_gather(mean, "tm", axis=0, tiled=True)
    local_weighted = (root[None, :] * (snapshots.astype(jnp.float32) - all_means[None, :])).astype(
        jnp.bfloat16
    )
    own_rows = lax.dynamic_slice_in_dim(eigvecs, tm_index * time_dev, time_dev, 0)
    summed = lax.psum_scatter(
        jnp.dot(own_rows.T, local_weighted, preferred_element_type=jnp.float32),
        "tm",
        scatter_dimension=0,
        tiled=True,
    )
    own_scale = lax.dynamic_slice_in_dim(inv_root, tm_index * mode_dev, mode_dev, 0)
    modes = (summed * own_scale[:, None]).astype(jnp.bfloat16)
    return (gram, modes)


def solution(mesh):
    in_specs = (P("tm", "space"), P("space"), P(), P())
    out_specs = (P(("tm", "space"), None), P("tm", "space"))
    return jax.shard_map(local, mesh=mesh, in_specs=in_specs, out_specs=out_specs, check_vma=False)
```

profile of v0, /device:TPU:1, one launch (start us, length us, event | category | flops | bytes accessed | tf_op | source)
XLA Modules:
  0.0 477.4 jit_solution(4174322892892114167)
XLA Ops:
  7.2 0.0 copy-start
  7.2 16.5 %copy.8 = bf16[128,49152]{0,1:T(8,128)(2,1)} copy(bf16[128,49152]{1,0:T(8,128)(2,1)} %param.4) | data formatting | bytes 25165824 | tf_op args[0]
  23.7 7.0 %all-to-all-start = ((bf16[128,8,6144]{0,2,1:T(8,128)(2,1)}), bf16[128,8,6144]{0,2,1:T(8,128)(2,1)}, u32[]{:S(2)}, u32[]{:S(2)}) async-start(bf16[128,8,6144]{0,2,1:T(8,128)(2,1)} %bitcast.6), calls=%async_computation | async-start | bytes 25165824 | tf_op jit(solution)/shard_map/all_to_all | solution.py:23
  30.7 0.0 reduce-scatter.4.cloned.1.call-start
  30.7 0.1 sqrt.6
  30.8 139.1 %all-to-all-done = bf16[128,8,6144]{0,2,1:T(8,128)(2,1)} async-done(((bf16[128,8,6144]{0,2,1:T(8,128)(2,1)}), bf16[128,8,6144]{0,2,1:T(8,128)(2,1)}, u32[]{:S(2)}, u32[]{:S(2)}) %all-to-all-start) | async-done | bytes 12582944 | tf_op jit(solution)/shard_map/all_to_all | solution.py:23
  169.9 6.3 %convert_reduce_fusion = f32[6144]{0:T(1024)S(1)} fusion(bf16[128,8,6144]{0,2,1:T(8,128)(2,1)} %all-to-all-done), kind=kLoop, calls=%fused_computation.1 | loop fusion | flops 12576768 | bytes 12607488 | tf_op jit(solution)/shard_map/reduce_sum | solution.py:24
  176.2 11.9 %fusion.3 = bf16[8,128,6144]{1,2,0:T(8,128)(2,1)} fusion(bf16[128,8,6144]{0,2,1:T(8,128)(2,1)} %all-to-all-done, f32[6144]{0:T(1024)S(1)} %broadcast_multiply_fusion, f32[6144]{0:T(1024)S(1)} %dynamic_slice.9), kind=kLoop, calls=%fused_computation.6 | loop fusion | flops 25165824 | bytes 25214976 | tf_op jit(solution)/shard_map/convert_element_type | solution.py:27
  188.1 16.7 %copy.9 = bf16[8,128,6144]{2,1,0:T(8,128)(2,1)} copy(bf16[8,128,6144]{1,2,0:T(8,128)(2,1)} %fusion.3) | data formatting | bytes 25165824 | tf_op jit(solution)/shard_map/convert_element_type | solution.py:27
  204.8 19.1 %multiply_convert_fusion.2 = bf16[1024,1024]{1,0:T(8,128)(2,1)} fusion(bf16[1024,6144]{1,0:T(8,128)(2,1)} %bitcast.7), kind=kOutput, calls=%fused_computation.9 | convolution fusion | flops 12886999040 | bytes 14680064 | tf_op jit(solution)/shard_map/dot_general | solution.py:8
  223.8 0.0 reduce-scatter.4.cloned.1.call-update
  223.9 0.0 reduce-scatter.6.cloned.1.call-start
  223.9 23.4 %all_gather.3 = f32[49152]{0:T(1024)S(1)} all-gather(f32[6144]{0:T(1024)S(1)} %broadcast_multiply_fusion), channel_id=1, replica_groups=mesh['tm'=8,'space'=16] {'tm'}, dimensions={0}, use_global_device_ids=true | all-gather | bytes 221184 | tf_op jit(solution)/shard_map/all_gather | solution.py:36
  247.3 14.6 %reduce-scatter.4.cloned.1.call-done = bf16[128,1024]{1,0:T(8,128)(2,1)} async-done(((bf16[1024,1024]{1,0:T(8,128)(2,1)}), bf16[128,1024]{1,0:T(8,128)(2,1)}) %reduce-scatter.4.cloned.1.call-update) | async-done | bytes 262160 | tf_op jit(solution)/shard_map/reduce_scatter | solution.py:31
  261.9 0.0 reduce-scatter.6.cloned.1.call-update
  261.9 0.0 reduce-scatter.8.cloned.1.call-start
  262.0 13.2 %fusion.2 = f32[64,49152]{1,0:T(8,128)} fusion(bf16[128,49152]{1,0:T(8,128)(2,1)} %param.4, f32[49152]{0:T(1024)S(1)} %all_gather.3, f32[49152]{0:T(1024)S(1)} %sqrt.6, bf16[1024,64]{0,1:T(8,128)(2,1)S(1)} %copy-done, s32[]{:T(128)S(6)} %select_n.10), kind=kOutput, calls=%fused_computation.5 | convolution fusion | flops 830472192 | bytes 25575428 | tf_op jit(solution)/shard_map/dot_general | solution.py:42
  275.2 0.0 reduce-scatter.8.cloned.1.call-update
  275.2 0.6 copy-done.2
  275.8 0.1 dynamic_slice.11
  275.9 56.3 %reduce-scatter.6.cloned.1.call-done = bf16[8,1024]{1,0:T(8,128)(2,1)} async-done(((bf16[128,1024]{1,0:T(8,128)(2,1)}), bf16[8,1024]{1,0:T(8,128)(2,1)}) %reduce-scatter.6.cloned.1.call-update) | async-done | bytes 16400 | tf_op jit(solution)/shard_map/reduce_scatter | solution.py:34
  332.2 1.3 convert_element_type.38
  333.6 134.8 %reduce-scatter.8.cloned.1.call-done = f32[8,49152]{1,0:T(8,128)} async-done(((f32[64,49152]{1,0:T(8,128)}), f32[8,49152]{1,0:T(8,128)}) %reduce-scatter.8.cloned.1.call-update) | async-done | bytes 1572880 | tf_op jit(solution)/shard_map/reduce_scatter | solution.py:41
  468.4 2.4 multiply_convert_fusion.3
  (7 shorter events, 0.0 us)
Async XLA Ops:
  7.2 254.8 %copy-start = (bf16[1024,64]{0,1:T(8,128)(2,1)S(1)}, bf16[1024,64]{0,1:T(8,128)(2,1)}, u32[]{:S(2)}) copy-start(bf16[1024,64]{0,1:T(8,128)(2,1)} %param.6) | copy-start | bytes 393220
  23.7 7.1 %copy-start.1 = (f32[49152]{0:T(1024)S(1)}, f32[49152]{0:T(1024)}, u32[]{:S(2)}) copy-start(f32[49152]{0:T(1024)} %param.5) | copy-start | bytes 589828
  23.7 146.3 %all-to-all-start = ((bf16[128,8,6144]{0,2,1:T(8,128)(2,1)}), bf16[128,8,6144]{0,2,1:T(8,128)(2,1)}, u32[]{:S(2)}, u32[]{:S(2)}) async-start(bf16[128,8,6144]{0,2,1:T(8,128)(2,1)} %bitcast.6), calls=%async_computation | async-start | bytes 25165824 | tf_op jit(solution)/shard_map/all_to_all | solution.py:23
  30.7 231.2 %reduce-scatter.4.cloned.1.call-start = ((), (), s32[]{:S(2)}) async-start(), calls=%async_computation.4 | async-start | bytes 2359296 | tf_op jit(solution)/shard_map/reduce_scatter | solution.py:31
  223.9 108.4 %reduce-scatter.6.cloned.1.call-start = ((), (), s32[]{:S(2)}) async-start(), calls=%async_computation.5 | async-start | bytes 278528 | tf_op jit(solution)/shard_map/reduce_scatter | solution.py:34
  261.9 206.5 %reduce-scatter.8.cloned.1.call-start = ((), (), s32[]{:S(2)}) async-start(), calls=%async_computation.6 | async-start | bytes 14155776 | tf_op jit(solution)/shard_map/reduce_scatter | solution.py:41
  275.2 0.7 copy-start.2
Sparse Core Ops, SparseCore 0:
  224.0 37.8 reduce-scatter.3
  265.6 66.5 reduce-scatter.5
  334.8 133.5 reduce-scatter.7
where the time goes:
time: 479 us; the launch traced here: 477 us
  waiting for transfers between devices  345 us (72%)
  local copies, waits for them, and re-layouts  33.9 us (7%)
  matrix products  32.3 us (7%)
  blocking collectives  23.4 us (5%)
  other arithmetic  21.9 us (5%)
  between operations  13.8 us (3%)
  starting transfers between devices  7.12 us (1%)
    all_to_all x1, waiting for transfers between devices, local(): lax.all_to_all(snapshots, 'tm', split_axis=1, concat_axis=0, tiled=True)  139 us
    reduce_scatter x1, waiting for transfers between devices, local(): lax.psum_scatter(jnp.dot(own_rows.T, local_weighted, preferred_element_ty...  135 us
    reduce_scatter x1, waiting for transfers between devices, local(): lax.psum_scatter(row_sums, 'space', scatter_dimension=0, tiled=True)  56.3 us
    all_gather x1, blocking collectives, local(): all_means = lax.all_gather(mean, 'tm', axis=0, tiled=True)  23.4 us
    dot_general x1, matrix products, gram_local(): lax.dot_general(weighted, weighted, (((1,), (1,)), ((), ())), preferred_e...  19.1 us
    unnamed x7, local copies, waits for them, and re-layouts  17.1 us
    convert_element_type x1, local copies, waits for them, and re-layouts, local(): (own_root[None, :] * (columns.astype(jnp.float32) - mean[None, :])).astyp...  16.7 us
    reduce_scatter x1, waiting for transfers between devices, local(): lax.psum_scatter(partial_gram.astype(jnp.bfloat16), 'tm', scatter_dimensi...  14.6 us
  transfers between devices with their start and end apart: 4, of which 4 were waited for; matrix products, arithmetic and copies ran while one was open for 3% of the time, Pallas kernels for 0%

commit v1 on v0

v1 whole, which is shorter than its diff:
```python
import functools

import jax
import jax.numpy as jnp
from jax import lax
from jax.experimental import pallas as pl
from jax.experimental.pallas import tpu as pltpu
from jax.sharding import PartitionSpec as P

MESH = pl.DeviceIdType.MESH
CHUNKS = 8
AHEAD = 3


def kernel(snap, area, evt, evals, gram_out, modes_out,
           buf, wbuf, acc, inv, area_v, msend, csend, crecv, xsend, xrecv, part, ysend, yrecv,
           s_send, s_recv, s_own, s_area, m_send, m_recv, m_own,
           c_send, c_recv, x_send, x_recv, y_send, y_recv):
    time_dev, cell_dev = snap.shape
    times, sub = buf.shape
    width = wbuf.shape[1]
    modes_n = evt.shape[0]
    cells = cell_dev * 16
    half = times // 2

    tm = lax.axis_index("tm")
    sp = lax.axis_index("space")
    y_lo, z = tm // 4, lax.rem(tm, 4)
    y_hi, x, core = sp // 8, lax.rem(sp // 2, 4), lax.rem(sp, 2)

    def tm_of(j, sign):
        return lax.rem(y_lo + j // 4, 2) * 4 + lax.rem(z + sign * (j % 4) + 4, 4)

    def sp_x(dx, sign):
        return y_hi * 8 + lax.rem(x + sign * dx + 4, 4) * 2 + core

    def yz_of(j, sign):
        return tm_of(j % 8, sign), lax.rem(y_hi + j // 8, 2)

    def yz_dev(j, sign):
        t, h = yz_of(j, sign)
        return (t, h * 8 + x * 2 + core)

    other = (tm, sp + 1 - 2 * core)

    barrier = pltpu.get_barrier_semaphore()
    partners = [yz_dev(j, 1) for j in range(1, 16)] + [other] + [(tm, sp_x(d, 1)) for d in (1, 2, 3)]
    for device in partners:
        pl.semaphore_signal(barrier, inc=1, device_id=device, device_id_type=MESH)
    pl.semaphore_wait(barrier, len(partners))

    def raw(k, j, sign):
        peer = tm_of(j, sign)
        cols = pl.ds(pl.multiple_of(k * width, 128), width)
        row = tm if sign > 0 else peer
        return pltpu.make_async_remote_copy(
            src_ref=snap.at[:, pl.ds(pl.multiple_of(peer * sub + k * width, 128), width)],
            dst_ref=buf.at[pl.ds(pl.multiple_of(row * time_dev, 128), time_dev), cols],
            send_sem=s_send.at[k, j - 1], recv_sem=s_recv.at[k, j - 1],
            device_id=(peer, sp), device_id_type=MESH)

    own_copy = pltpu.make_async_copy(
        snap.at[:, pl.ds(pl.multiple_of(tm * sub, 128), sub)],
        buf.at[pl.ds(pl.multiple_of(tm * time_dev, 128), time_dev), :], s_own)
    area_rows = sub // 128
    area_copy = pltpu.make_async_copy(
        area.at[pl.ds(pl.multiple_of(tm * area_rows, 8), area_rows), :], area_v, s_area)

    def start_chunk(k):
        for j in range(1, 8):
            raw(k, j, 1).start()

    for k in range(AHEAD):
        start_chunk(k)
    own_copy.start()
    area_copy.start()

    acc[...] = jnp.zeros_like(acc)
    eye = lax.broadcasted_iota(jnp.int32, (modes_n, modes_n), 0) == lax.broadcasted_iota(
        jnp.int32, (modes_n, modes_n), 1)
    inv[...] = 1.0 / jnp.sqrt(jnp.sum(
        jnp.where(eye, jnp.broadcast_to(evals[...], (modes_n, modes_n)), 0.0), axis=1, keepdims=True))
    area_copy.wait()
    area_v[...] = jnp.sqrt(area_v[...])
    own_copy.wait()

    strips = width // 128

    def chunk(k, carry):
        for j in range(1, 8):
            raw(k, j, -1).wait_recv()
        for j in range(1, 8):
            raw(k, j, 1).wait_send()

        @pl.when(k + AHEAD < CHUNKS)
        def _():
            start_chunk(k + AHEAD)

        base = pl.multiple_of(k * width, 128)
        cols = pl.ds(base, width)

        def add(i, total):
            block = buf[pl.ds(pl.multiple_of(i * 64, 64), 64), cols].astype(jnp.float32)
            return total + jnp.sum(block.reshape(8, 8, width), axis=0)

        total = lax.fori_loop(0, times // 64, add, jnp.zeros((8, width), jnp.float32))
        mean = jnp.sum(total, axis=0, keepdims=True) / times
        root = jnp.concatenate(
            [area_v[pl.ds(k * strips + s, 1), :] for s in range(strips)], axis=1)

        def weigh(i, c):
            rows = pl.ds(pl.multiple_of(i * 64, 64), 64)
            block = buf[rows, cols].astype(jnp.float32)
            wbuf[rows, :] = (root * (block - mean)).astype(jnp.bfloat16)
            return c

        lax.fori_loop(0, times // 64, weigh, 0)

        def gram(i, c):
            tile = pl.ds(pl.multiple_of(i * 256, 256), 256)
            acc[:, tile] += lax.dot_general(
                wbuf[...], wbuf[tile, :], (((1,), (1,)), ((), ())),
                preferred_element_type=jnp.float32)
            return c

        lax.fori_loop(0, times // 256, gram, 0)
        proj = jnp.dot(evt[...], wbuf[...], preferred_element_type=jnp.float32) * inv[...]
        proj = proj.astype(jnp.bfloat16)
        for p in range(8):
            msend[p, :, cols] = proj[p * 8:p * 8 + 8, :]
        return carry

    lax.fori_loop(0, CHUNKS, chunk, 0)

    own_cols = pl.ds(pl.multiple_of(tm * sub, 128), sub)

    def modes_copy(j, sign):
        peer = tm_of(j, sign)
        col = tm if sign > 0 else peer
        return pltpu.make_async_remote_copy(
            src_ref=msend.at[peer],
            dst_ref=modes_out.at[:, pl.ds(pl.multiple_of(col * sub, 128), sub)],
            send_sem=m_send.at[j - 1], recv_sem=m_recv.at[j - 1],
            device_id=(peer, sp), device_id_type=MESH)

    for j in range(1, 8):
        modes_copy(j, 1).start()
    modes_own = pltpu.make_async_copy(msend.at[tm], modes_out.at[:, own_cols], m_own)
    modes_own.start()

    def unit(g, dx, which):
        at = ((g * 4 + lax.rem(x + dx, 4)) * 2 + which) * 8
        rows = acc[pl.ds(pl.multiple_of(at, 8), 8), :]
        return jnp.concatenate([rows[:, :half], rows[:, half:]], axis=0)

    def core_copy(dx):
        return pltpu.make_async_remote_copy(
            src_ref=csend.at[dx], dst_ref=crecv.at[dx],
            send_sem=c_send.at[dx], recv_sem=c_recv.at[dx],
            device_id=other, device_id_type=MESH)

    def x_copy(dx, sign):
        return pltpu.make_async_remote_copy(
            src_ref=xsend.at[dx - 1], dst_ref=xrecv.at[dx - 1],
            send_sem=x_send.at[dx - 1], recv_sem=x_recv.at[dx - 1],
            device_id=(tm, sp_x(dx, sign)), device_id_type=MESH)

    order = (2, 1, 3, 0)
    for dx in order:
        def pack(g, c, dx=dx):
            csend[dx, g] = unit(g, dx, 1 - core).astype(jnp.bfloat16)
            return c
        lax.fori_loop(0, 16, pack, 0)
        core_copy(dx).start()

    for dx in order:
        core_copy(dx).wait_recv()

        def merge(g, c, dx=dx):
            value = unit(g, dx, core) + crecv[dx, g].astype(jnp.float32)
            if dx:
                xsend[dx - 1, g] = value.astype(jnp.bfloat16)
            else:
                part[g] = value
            return c
        lax.fori_loop(0, 16, merge, 0)
        if dx:
            x_copy(dx, 1).start()
    for dx in (1, 2, 3):
        x_copy(dx, -1).wait_recv()

    def merge_x(g, c):
        value = part[g]
        for d in range(3):
            value = value + xrecv[d, g].astype(jnp.float32)
        part[g] = value
        ysend[g] = value.astype(jnp.bfloat16)
        return c
    lax.fori_loop(0, 16, merge_x, 0)

    def y_copy(j, sign):
        t, h = yz_of(j, sign)
        return pltpu.make_async_remote_copy(
            src_ref=ysend.at[t * 2 + h], dst_ref=yrecv.at[j - 1],
            send_sem=y_send.at[j - 1], recv_sem=y_recv.at[j - 1],
            device_id=(t, h * 8 + x * 2 + core), device_id_type=MESH)

    for j in range(1, 16):
        y_copy(j, 1).start()
    total = part[tm * 2 + y_hi]
    for j in range(1, 16):
        y_copy(j, -1).wait_recv()
        total = total + yrecv[j - 1].astype(jnp.float32)
    total = total / cells
    gram_out[:, :half] = total[:8, :]
    gram_out[:, half:] = total[8:, :]

    modes_own.wait()
    for j in range(1, 8):
        modes_copy(j, -1).wait_recv()
        modes_copy(j, 1).wait_send()
    for dx in range(4):
        core_copy(dx).wait_send()
    for dx in (1, 2, 3):
        x_copy(dx, 1).wait_send()
    for j in range(1, 16):
        y_copy(j, 1).wait_send()


def local(snapshots, area_weight, eigvecs, eigvals):
    tm_count = lax.axis_size("tm")
    time_dev, cell_dev = snapshots.shape
    times = time_dev * tm_count
    sub = cell_dev // tm_count
    modes_n = eigvecs.shape[1]
    width = sub // CHUNKS
    vmem = pl.BlockSpec(memory_space=pltpu.VMEM)
    hbm = pl.BlockSpec(memory_space=pl.ANY)
    bf16, f32 = jnp.bfloat16, jnp.float32
    half = times // 2
    dma = pltpu.SemaphoreType.DMA
    return pl.pallas_call(
        kernel,
        out_shape=(jax.ShapeDtypeStruct((8, times), f32), jax.ShapeDtypeStruct((8, cell_dev), bf16)),
        in_specs=[hbm, hbm, vmem, vmem],
        out_specs=(vmem, hbm),
        scratch_shapes=[
            pltpu.VMEM((times, sub), bf16),
            pltpu.VMEM((times, width), bf16),
            pltpu.VMEM((times, times), f32),
            pltpu.VMEM((modes_n, 1), f32),
            pltpu.VMEM((sub // 128, 128), f32),
            pltpu.VMEM((tm_count, 8, sub), bf16),
            pltpu.VMEM((4, 16, 16, half), bf16),
            pltpu.VMEM((4, 16, 16, half), bf16),
            pltpu.VMEM((3, 16, 16, half), bf16),
            pltpu.VMEM((3, 16, 16, half), bf16),
            pltpu.VMEM((16, 16, half), f32),
            pltpu.VMEM((16, 16, half), bf16),
            pltpu.VMEM((15, 16, half), bf16),
            dma((CHUNKS, 7)), dma((CHUNKS, 7)), dma, dma,
            dma((7,)), dma((7,)), dma,
            dma((4,)), dma((4,)), dma((3,)), dma((3,)), dma((15,)), dma((15,)),
        ],
        compiler_params=pltpu.CompilerParams(
            collective_id=0, has_side_effects=True, vmem_limit_bytes=48 << 20),
        cost_estimate=pl.CostEstimate(
            flops=2 * times * times * sub, bytes_accessed=2 * times * sub, transcendentals=0),
    )(snapshots, area_weight.reshape(-1, 128), eigvecs.T, eigvals.reshape(1, -1))


def solution(mesh):
    in_specs = (P("tm", "space"), P("space"), P(), P())
    out_specs = (P(("tm", "space"), None), P("tm", "space"))
    return jax.shard_map(local, mesh=mesh, in_specs=in_specs, out_specs=out_specs, check_vma=False)
```

time: 479 us -> 182 us (0.38)
  waiting for transfers between devices: 345 us -> 0 us
  Pallas kernels: 0 us -> 177 us
  matrix products: 32.3 us -> 0 us
  local copies, waits for them, and re-layouts: 33.9 us -> 3.97 us
  blocking collectives: 23.4 us -> 0 us
  other arithmetic: 21.9 us -> 0 us
  between operations: 13.8 us -> 0.65 us
  starting transfers between devices: 7.12 us -> 0 us
    reduce_scatter x3 -> x0, waiting for transfers between devices: 206 us -> none  [the longest x1 135 us: local(): lax.psum_scatter(jnp.dot(own_rows.T, local_weighted, preferred_element_ty...]
    pallas_call x0 -> x1, Pallas kernels: none -> 177 us  [local(): pl.pallas_call(kernel, out_shape=(jax.ShapeDtypeStruct((8, times), f32),...]
    all_to_all x1 -> x0, waiting for transfers between devices: 139 us -> none  [local(): lax.all_to_all(snapshots, 'tm', split_axis=1, concat_axis=0, tiled=True)]
    dot_general x2 -> x0, matrix products: 32.3 us -> none  [the longest x1 19.1 us: gram_local(): lax.dot_general(weighted, weighted, (((1,), (1,)), ((), ())), preferred_e...]
    all_gather x1 -> x0, blocking collectives: 23.4 us -> none  [local(): all_means = lax.all_gather(mean, 'tm', axis=0, tiled=True)]
    convert_element_type x1 -> x0, local copies, waits for them, and re-layouts: 16.7 us -> none  [local(): (own_root[None, :] * (columns.astype(jnp.float32) - mean[None, :])).astyp...]
    convert_element_type x3 -> x0, other arithmetic: 15.6 us -> none  [the longest x1 11.9 us: local(): (own_root[None, :] * (columns.astype(jnp.float32) - mean[None, :])).astyp...]
    unnamed x7 -> x8, local copies, waits for them, and re-layouts: 17.1 us -> 3.97 us
  transfers between devices with their start and end apart: 4 -> 0, of which waited for: 4 -> 0; matrix products, arithmetic and copies ran while one was open for 3% -> 0% of each run, Pallas kernels for 0% -> 0%
where the time goes in v1:
time: 182 us
  Pallas kernels  177 us (97%)
  local copies, waits for them, and re-layouts  3.97 us (2%)
    pallas_call x1, Pallas kernels, local(): pl.pallas_call(kernel, out_shape=(jax.ShapeDtypeStruct((8, times), f32),...  177 us
    unnamed x8, local copies, waits for them, and re-layouts  3.97 us

profile of v1, /device:TPU:1, one launch (start us, length us, event | category | flops | bytes accessed | tf_op | source)
XLA Modules:
  0.0 181.6 jit_solution(10238569289980708047)
XLA Ops:
  0.6 0.0 copy-start
  0.6 0.9 copy-done
  1.6 0.0 copy-start.1
  1.6 0.9 copy-done.1
  2.5 0.0 copy-start.2
  2.5 0.7 copy-done.2
  3.1 177.0 %shard_map.59 = (f32[8,1024]{1,0:T(8,128)S(1)}, bf16[8,49152]{1,0:T(8,128)(2,1)S(1)}) custom-call(bf16[128,49152]{1,0:T(8,128)(2,1)} %snap.1, f32[384,128]{1,0:T(8,128)S(1)} %bitcast.3, bf16[64,1024]{1,0:T(8,128)(2,1)S(1)} %bitcast.4, f32[1,64]{1,0:T(1,128)S(1)} %bitcast.5), custom_call_target="tpu_custom_call" | custom-call | flops 12884901888 | bytes 12582912 | tf_op jit(solution)/shard_map/pallas_call | solution.py:242
  180.1 0.6 copy.8
  180.8 0.9 copy.9
Async XLA Ops:
  0.6 0.9 copy-start
  1.6 0.9 copy-start.1
  2.5 0.7 copy-start.2

commit v2 on v1

--- a/solution.py
+++ b/solution.py
@@ -8,13 +8,13 @@
 from jax.sharding import PartitionSpec as P
 
 MESH = pl.DeviceIdType.MESH
-CHUNKS = 8
-AHEAD = 3
-
-
-def kernel(snap, area, evt, evals, gram_out, modes_out,
-           buf, wbuf, acc, inv, area_v, msend, csend, crecv, xsend, xrecv, part, ysend, yrecv,
-           s_send, s_recv, s_own, s_area, m_send, m_recv, m_own,
+CHUNKS = 12
+AHEAD = 4
+
+
+def kernel(snap, area, evt_in, evals_in, gram_out, modes_out,
+           buf, wbuf, acc, evt, evals, inv, area_v, msend, csend, crecv, xsend, xrecv, part, ysend, yrecv,
+           s_send, s_recv, s_own, s_area, s_evt, s_evals, m_send, m_recv, m_own,
            c_send, c_recv, x_send, x_recv, y_send, y_recv):
     time_dev, cell_dev = snap.shape
     times, sub = buf.shape
@@ -74,8 +74,14 @@
         start_chunk(k)
     own_copy.start()
     area_copy.start()
+    evt_copy = pltpu.make_async_copy(evt_in, evt, s_evt)
+    evals_copy = pltpu.make_async_copy(evals_in, evals, s_evals)
+    evals_copy.start()
+    evt_copy.start()
 
     acc[...] = jnp.zeros_like(acc)
+    evals_copy.wait()
+    evt_copy.wait()
     eye = lax.broadcasted_iota(jnp.int32, (modes_n, modes_n), 0) == lax.broadcasted_iota(
         jnp.int32, (modes_n, modes_n), 1)
     inv[...] = 1.0 / jnp.sqrt(jnp.sum(
@@ -235,19 +241,21 @@
     modes_n = eigvecs.shape[1]
     width = sub // CHUNKS
     vmem = pl.BlockSpec(memory_space=pltpu.VMEM)
-    hbm = pl.BlockSpec(memory_space=pl.ANY)
+    hbm = pl.BlockSpec(memory_space=pltpu.HBM)
     bf16, f32 = jnp.bfloat16, jnp.float32
     half = times // 2
     dma = pltpu.SemaphoreType.DMA
     return pl.pallas_call(
         kernel,
         out_shape=(jax.ShapeDtypeStruct((8, times), f32), jax.ShapeDtypeStruct((8, cell_dev), bf16)),
-        in_specs=[hbm, hbm, vmem, vmem],
+        in_specs=[hbm] * 4,
         out_specs=(vmem, hbm),
         scratch_shapes=[
             pltpu.VMEM((times, sub), bf16),
             pltpu.VMEM((times, width), bf16),
             pltpu.VMEM((times, times), f32),
+            pltpu.VMEM((modes_n, times), bf16),
+            pltpu.VMEM((1, modes_n), f32),
             pltpu.VMEM((modes_n, 1), f32),
             pltpu.VMEM((sub // 128, 128), f32),
             pltpu.VMEM((tm_count, 8, sub), bf16),
@@ -258,12 +266,12 @@
             pltpu.VMEM((16, 16, half), f32),
             pltpu.VMEM((16, 16, half), bf16),
             pltpu.VMEM((15, 16, half), bf16),
-            dma((CHUNKS, 7)), dma((CHUNKS, 7)), dma, dma,
+            dma((CHUNKS, 7)), dma((CHUNKS, 7)), dma, dma, dma, dma,
             dma((7,)), dma((7,)), dma,
             dma((4,)), dma((4,)), dma((3,)), dma((3,)), dma((15,)), dma((15,)),
         ],
         compiler_params=pltpu.CompilerParams(
-            collective_id=0, has_side_effects=True, vmem_limit_bytes=48 << 20),
+            collective_id=0, has_side_effects=True, vmem_limit_bytes=62 << 20),
         cost_estimate=pl.CostEstimate(
             flops=2 * times * times * sub, bytes_accessed=2 * times * sub, transcendentals=0),
     )(snapshots, area_weight.reshape(-1, 128), eigvecs.T, eigvals.reshape(1, -1))

time: 182 us -> 178 us (0.978)
  Pallas kernels: 177 us -> 174 us
    pallas_call x1, Pallas kernels: 177 us -> 174 us  [local(): pl.pallas_call(kernel, out_shape=(jax.ShapeDtypeStruct((8, times), f32),...]
    unnamed x8 -> x2, local copies, waits for them, and re-layouts: 3.97 us -> 3.44 us
where the time goes in v2:
time: 178 us
  Pallas kernels  174 us (98%)
  local copies, waits for them, and re-layouts  3.44 us (2%)
    pallas_call x1, Pallas kernels, local(): pl.pallas_call(kernel, out_shape=(jax.ShapeDtypeStruct((8, times), f32),...  174 us

profile of v2, /device:TPU:1, one launch (start us, length us, event | category | flops | bytes accessed | tf_op | source)
XLA Modules:
  0.0 177.7 jit_solution(7370566464172472740)
XLA Ops:
  0.6 173.6 %shard_map.59 = (f32[8,1024]{1,0:T(8,128)}, bf16[8,49152]{1,0:T(8,128)(2,1)}) custom-call(bf16[128,49152]{1,0:T(8,128)(2,1)} %snap.1, f32[384,128]{1,0:T(8,128)} %bitcast.3, bf16[64,1024]{1,0:T(8,128)(2,1)} %bitcast.4, f32[1,64]{1,0:T(1,128)} %bitcast.5), custom_call_target="tpu_custom_call" | custom-call | flops 12884901888 | bytes 12582912 | tf_op jit(solution)/shard_map/pallas_call | solution.py:248
  174.2 1.4 copy.8
  175.6 2.1 %copy.9 = bf16[8,49152]{1,0:T(8,128)(2,1)} copy(bf16[8,49152]{1,0:T(8,128)(2,1)} %get-tuple-element.5) | data formatting | bytes 1572864

commit v3 on v2

v3 whole, which is shorter than its diff:
```python
import jax
import jax.numpy as jnp
from jax import lax
from jax.experimental import pallas as pl
from jax.experimental.pallas import tpu as pltpu
from jax.sharding import PartitionSpec as P

MESH = pl.DeviceIdType.MESH
CHUNKS = 12
AHEAD = 4
FIRST = (1, 2, 3, 4, 5, 7)
LAST = 6
BF16, F32 = jnp.bfloat16, jnp.float32


def kernel(snap, area, evt_in, evals_in, gram_out, modes_out,
           buf, abuf, sbuf, asum, asum_in, means, acc, late, lrow, evt, evals, inv, area_v, mpart, msend,
           csend, crecv, xsend, xrecv, part, ysend, yrecv,
           ltc, ltc_in, lrc, lrc_in, ltx, ltx_in, lrx, lrx_in,
           s_send, s_recv, a_send, a_recv, t_send, t_recv, s_local, m_send, m_recv, m_own,
           c_send, c_recv, x_send, x_recv, y_send, y_recv, lc_send, lc_recv, lx_send, lx_recv):
    time_dev, cell_dev = snap.shape
    times, sub = buf.shape
    width = sub // CHUNKS
    modes_n = evt.shape[0]
    cells = cell_dev * 16
    half = times // 2

    tm = lax.axis_index("tm")
    sp = lax.axis_index("space")
    y_lo, z = tm // 4, lax.rem(tm, 4)
    y_hi, x, core = sp // 8, lax.rem(sp // 2, 4), lax.rem(sp, 2)

    def tm_of(j, sign):
        return lax.rem(y_lo + j // 4, 2) * 4 + lax.rem(z + sign * (j % 4) + 4, 4)

    def sp_x(dx, sign):
        return y_hi * 8 + lax.rem(x + sign * dx + 4, 4) * 2 + core

    def yz_of(j, sign):
        return tm_of(j % 8, sign), lax.rem(y_hi + j // 8, 2)

    def yz_dev(j, sign):
        t, h = yz_of(j, sign)
        return (t, h * 8 + x * 2 + core)

    def rcopy(src, dst, send, recv, device):
        return pltpu.make_async_remote_copy(
            src_ref=src, dst_ref=dst, send_sem=send, recv_sem=recv,
            device_id=device, device_id_type=MESH)

    other = (tm, sp + 1 - 2 * core)
    anti = tm_of(LAST, 1)

    barrier = pltpu.get_barrier_semaphore()
    partners = [yz_dev(j, 1) for j in range(1, 16)] + [other] + [(tm, sp_x(d, 1)) for d in (1, 2, 3)]
    for device in partners:
        pl.semaphore_signal(barrier, inc=1, device_id=device, device_id_type=MESH)
    pl.semaphore_wait(barrier, len(partners))

    def columns(k):
        return pl.ds(pl.multiple_of(k * width, 128), width)

    def block_rows(t):
        return pl.ds(pl.multiple_of(t * time_dev, 128), time_dev)

    def raw(k, i, sign):
        peer = tm_of(FIRST[i], sign)
        row = tm if sign > 0 else peer
        return rcopy(snap.at[:, pl.ds(pl.multiple_of(peer * sub + k * width, 128), width)],
                     buf.at[block_rows(row), columns(k)],
                     s_send.at[k, i], s_recv.at[k, i], (peer, sp))

    def raw_anti(k):
        return rcopy(snap.at[:, pl.ds(pl.multiple_of(anti * sub + k * width, 128), width)],
                     abuf.at[:, columns(k)], a_send.at[k], a_recv.at[k], (anti, sp))

    def start_chunk(k):
        for i in range(len(FIRST)):
            raw(k, i, 1).start()

    area_rows = sub // 128
    local_copies = [pltpu.make_async_copy(src, dst, s_local.at[i]) for i, (src, dst) in enumerate((
        (snap.at[:, pl.ds(pl.multiple_of(anti * sub, 128), sub)], sbuf),
        (snap.at[:, pl.ds(pl.multiple_of(tm * sub, 128), sub)], buf.at[block_rows(tm), :]),
        (area.at[pl.ds(pl.multiple_of(tm * area_rows, 8), area_rows), :], area_v),
        (evals_in, evals),
        (evt_in, evt),
    ))]
    start_chunk(0)
    for copy in local_copies:
        copy.start()
    for k in range(1, AHEAD):
        start_chunk(k)

    local_copies[0].wait()

    def share(k, c):
        asum[:, columns(k)] = jnp.sum(sbuf[:, columns(k)].astype(F32), axis=0, keepdims=True)
        return c
    lax.fori_loop(0, CHUNKS, share, 0)
    sum_copy = rcopy(asum, asum_in, t_send, t_recv, (anti, sp))
    sum_copy.start()

    acc[...] = jnp.zeros_like(acc)
    late[...] = jnp.zeros_like(late)

    def clear(i, c):
        buf[pl.ds(pl.multiple_of(anti * time_dev + i * 16, 16), 16), :] = jnp.zeros((16, sub), BF16)
        return c
    lax.fori_loop(0, time_dev // 16, clear, 0)
    for copy in local_copies[1:]:
        copy.wait()
    eye = lax.broadcasted_iota(jnp.int32, (modes_n, modes_n), 0) == lax.broadcasted_iota(
        jnp.int32, (modes_n, modes_n), 1)
    inv[...] = 1.0 / jnp.sqrt(jnp.sum(
        jnp.where(eye, jnp.broadcast_to(evals[...], (modes_n, modes_n)), 0.0), axis=1, keepdims=True))
    area_v[...] = jnp.sqrt(area_v[...])
    sum_copy.wait_recv()

    strips = width // 128

    def root_of(k):
        return jnp.concatenate([area_v[pl.ds(k * strips + s, 1), :] for s in range(strips)], axis=1)

    def nt_dot(a, b):
        return lax.dot_general(a, b, (((1,), (1,)), ((), ())), preferred_element_type=F32)

    def early_chunk(k, carry):
        for i in range(len(FIRST)):
            raw(k, i, -1).wait_recv()
        for i in range(len(FIRST)):
            raw(k, i, 1).wait_send()

        @pl.when(k + AHEAD < CHUNKS)
        def _():
            start_chunk(k + AHEAD)

        @pl.when(k + AHEAD >= CHUNKS)
        def _():
            raw_anti(k + AHEAD - CHUNKS).start()

        cols = columns(k)
        pieces = (times - time_dev) // 64

        def rows_of(i):
            return pl.ds(pl.multiple_of(lax.rem((anti + 1) * time_dev + i * 64, times), 64), 64)

        def add(i, total):
            block = buf[rows_of(i), cols].astype(F32)
            return total + jnp.sum(block.reshape(8, 8, width), axis=0)

        total = lax.fori_loop(0, pieces, add, jnp.zeros((8, width), F32))
        mean = (jnp.sum(total, axis=0, keepdims=True) + asum_in[:, cols]) / times
        means[:, cols] = mean
        root = root_of(k)

        def weigh(i, c):
            rows = rows_of(i)
            buf[rows, cols] = (root * (buf[rows, cols].astype(F32) - mean)).astype(BF16)
            return c
        lax.fori_loop(0, pieces, weigh, 0)

        def gram(i, c):
            tile = pl.ds(pl.multiple_of(i * 256, 256), 256)
            acc[:, tile] += nt_dot(buf[:, cols], buf[tile, cols])
            return c
        lax.fori_loop(0, times // 256, gram, 0)
        mpart[:, cols] = jnp.dot(evt[...], buf[:, cols], preferred_element_type=F32)
        return carry

    def late_chunk(k, carry):
        raw_anti(k).wait_recv()
        raw_anti(k).wait_send()

        @pl.when(k + AHEAD < CHUNKS)
        def _():
            raw_anti(k + AHEAD).start()

        cols = columns(k)
        weighted = (root_of(k) * (abuf[:, cols].astype(F32) - means[:, cols])).astype(BF16)
        buf[block_rows(anti), cols] = weighted
        late[...] += nt_dot(buf[:, cols], weighted)
        proj = mpart[:, cols] + jnp.dot(
            evt[:, block_rows(anti)], weighted, preferred_element_type=F32)
        proj = (proj * inv[...]).astype(BF16)
        for p in range(8):
            msend[p, :, cols] = proj[p * 8:p * 8 + 8, :]
        return carry

    def unit(ref, g, dx, which):
        at = ((g * 4 + lax.rem(x + dx, 4)) * 2 + which) * 8
        rows = ref[pl.ds(pl.multiple_of(at, 8), 8), :]
        return jnp.concatenate([rows[:, :half], rows[:, half:]], axis=0)

    def narrow(g, dx, which):
        at = ((g * 4 + lax.rem(x + dx, 4)) * 2 + which) * 8
        return late[pl.ds(pl.multiple_of(at, 8), 8), :]

    def core_copy(dx):
        return rcopy(csend.at[dx], crecv.at[dx], c_send.at[dx], c_recv.at[dx], other)

    def x_copy(dx, sign):
        return rcopy(xsend.at[dx - 1], xrecv.at[dx - 1], x_send.at[dx - 1], x_recv.at[dx - 1],
                     (tm, sp_x(dx, sign)))

    lax.fori_loop(0, CHUNKS, early_chunk, 0)

    order = (2, 1, 3, 0)
    for dx in order:
        def pack(g, c, dx=dx):
            csend[dx, g] = unit(acc, g, dx, 1 - core).astype(BF16)
            return c
        lax.fori_loop(0, 16, pack, 0)
        core_copy(dx).start()

    lax.fori_loop(0, 2, late_chunk, 0)

    for dx in order:
        core_copy(dx).wait_recv()

        def merge(g, c, dx=dx):
            value = unit(acc, g, dx, core) + crecv[dx, g].astype(F32)
            if dx:
                xsend[dx - 1, g] = value.astype(BF16)
            else:
                part[g] = value
            return c
        lax.fori_loop(0, 16, merge, 0)
        if dx:
            x_copy(dx, 1).start()

    lax.fori_loop(2, 9, late_chunk, 0)

    for dx in (1, 2, 3):
        x_copy(dx, -1).wait_recv()

    def merge_x(g, c):
        value = part[g]
        for d in range(3):
            value = value + xrecv[d, g].astype(F32)
        part[g] = value
        return c
    lax.fori_loop(0, 16, merge_x, 0)

    lax.fori_loop(9, CHUNKS, late_chunk, 0)

    def modes_copy(j, sign):
        peer = tm_of(j, sign)
        col = tm if sign > 0 else peer
        return rcopy(msend.at[peer], modes_out.at[:, pl.ds(pl.multiple_of(col * sub, 128), sub)],
                     m_send.at[j - 1], m_recv.at[j - 1], (peer, sp))

    for j in range(1, 8):
        modes_copy(j, 1).start()
    modes_own = pltpu.make_async_copy(
        msend.at[tm], modes_out.at[:, pl.ds(pl.multiple_of(tm * sub, 128), sub)], m_own)
    modes_own.start()

    lt_core = rcopy(ltc, ltc_in, lc_send.at[0], lc_recv.at[0], other)
    lr_core = rcopy(lrc, lrc_in, lc_send.at[1], lc_recv.at[1], other)

    def lt_x(dx, sign):
        return rcopy(ltx.at[dx - 1], ltx_in.at[dx - 1], lx_send.at[0, dx - 1], lx_recv.at[0, dx - 1],
                     (tm, sp_x(dx, sign)))

    def lr_x(dx, sign):
        return rcopy(lrx.at[dx - 1], lrx_in.at[dx - 1], lx_send.at[1, dx - 1], lx_recv.at[1, dx - 1],
                     (tm, sp_x(dx, sign)))

    def lt_pack(g, c):
        for dx in range(4):
            ltc[dx, g] = narrow(g, dx, 1 - core).astype(BF16)
        return c
    lax.fori_loop(0, 16, lt_pack, 0)
    lt_core.start()

    def turn(i, c):
        t = lax.rem(anti + 1 + i, 8)
        lrow[:, block_rows(t)] = jnp.transpose(late[block_rows(t), :])
        return c
    lax.fori_loop(0, 7, turn, 0)
    lrow[:, block_rows(anti)] = jnp.zeros((time_dev, time_dev), F32)
    for dx in range(4):
        for h in range(2):
            lrc[dx, h] = unit(lrow, h, dx, 1 - core).astype(BF16)
    lr_core.start()

    lane = pl.ds(pl.multiple_of(lax.rem(anti, 4) * 128, 128), 128)
    top = pl.ds(pl.multiple_of((anti // 4) * 8, 8), 8)

    lt_core.wait_recv()
    for dx in order:
        def lt_merge(g, c, dx=dx):
            value = narrow(g, dx, core) + ltc_in[dx, g].astype(F32)
            if dx:
                ltx[dx - 1, g] = value.astype(BF16)
            else:
                part[g, top, lane] += value
            return c
        lax.fori_loop(0, 16, lt_merge, 0)
        if dx:
            lt_x(dx, 1).start()
    lr_core.wait_recv()
    for dx in order:
        for h in range(2):
            value = unit(lrow, h, dx, core) + lrc_in[dx, h].astype(F32)
            if dx:
                lrx[dx - 1, h] = value.astype(BF16)
            else:
                part[anti * 2 + h] += value
        if dx:
            lr_x(dx, 1).start()
    for dx in (1, 2, 3):
        lt_x(dx, -1).wait_recv()

    def lt_sum(g, c):
        value = part[g, top, lane]
        for d in range(3):
            value = value + ltx_in[d, g].astype(F32)
        part[g, top, lane] = value
        return c
    lax.fori_loop(0, 16, lt_sum, 0)
    for dx in (1, 2, 3):
        lr_x(dx, -1).wait_recv()
    for h in range(2):
        value = part[anti * 2 + h]
        for d in range(3):
            value = value + lrx_in[d, h].astype(F32)
        part[anti * 2 + h] = value

    def y_copy(j, sign):
        t, h = yz_of(j, sign)
        return rcopy(ysend.at[t * 2 + h], yrecv.at[j - 1], y_send.at[j - 1], y_recv.at[j - 1],
                     (t, h * 8 + x * 2 + core))

    def y_pack(g, c):
        ysend[g] = part[g].astype(BF16)
        return c
    lax.fori_loop(0, 16, y_pack, 0)
    for j in range(1, 16):
        y_copy(j, 1).start()
    total = part[tm * 2 + y_hi]
    for j in range(1, 16):
        y_copy(j, -1).wait_recv()
        total = total + yrecv[j - 1].astype(F32)
    total = total / cells
    gram_out[:, :half] = total[:8, :]
    gram_out[:, half:] = total[8:, :]

    modes_own.wait()
    sum_copy.wait_send()
    for j in range(1, 8):
        modes_copy(j, -1).wait_recv()
        modes_copy(j, 1).wait_send()
    for dx in range(4):
        core_copy(dx).wait_send()
    lt_core.wait_send()
    lr_core.wait_send()
    for dx in (1, 2, 3):
        x_copy(dx, 1).wait_send()
        lt_x(dx, 1).wait_send()
        lr_x(dx, 1).wait_send()
    for j in range(1, 16):
        y_copy(j, 1).wait_send()


def local(snapshots, area_weight, eigvecs, eigvals):
    tm_count = lax.axis_size("tm")
    time_dev, cell_dev = snapshots.shape
    times = time_dev * tm_count
    sub = cell_dev // tm_count
    modes_n = eigvecs.shape[1]
    half = times // 2
    vmem = pl.BlockSpec(memory_space=pltpu.VMEM)
    hbm = pl.BlockSpec(memory_space=pltpu.HBM)
    dma = pltpu.SemaphoreType.DMA
    return pl.pallas_call(
        kernel,
        out_shape=(jax.ShapeDtypeStruct((8, times), F32), jax.ShapeDtypeStruct((8, cell_dev), BF16)),
        in_specs=[hbm] * 4,
        out_specs=(vmem, hbm),
        scratch_shapes=[
            pltpu.VMEM((times, sub), BF16),
            pltpu.VMEM((time_dev, sub), BF16),
            pltpu.VMEM((time_dev, sub), BF16),
            pltpu.VMEM((1, sub), F32),
            pltpu.VMEM((1, sub), F32),
            pltpu.VMEM((1, sub), F32),
            pltpu.VMEM((times, times), F32),
            pltpu.VMEM((times, time_dev), F32),
            pltpu.VMEM((time_dev, times), F32),
            pltpu.VMEM((modes_n, times), BF16),
            pltpu.VMEM((1, modes_n), F32),
            pltpu.VMEM((modes_n, 1), F32),
            pltpu.VMEM((sub // 128, 128), F32),
            pltpu.VMEM((modes_n, sub), F32),
            pltpu.VMEM((tm_count, 8, sub), BF16),
            pltpu.VMEM((4, 16, 16, half), BF16),
            pltpu.VMEM((4, 16, 16, half), BF16),
            pltpu.VMEM((3, 16, 16, half), BF16),
            pltpu.VMEM((3, 16, 16, half), BF16),
            pltpu.VMEM((16, 16, half), F32),
            pltpu.VMEM((16, 16, half), BF16),
            pltpu.VMEM((15, 16, half), BF16),
            pltpu.VMEM((4, 16, 8, 128), BF16),
            pltpu.VMEM((4, 16, 8, 128), BF16),
            pltpu.VMEM((4, 2, 16, half), BF16),
            pltpu.VMEM((4, 2, 16, half), BF16),
            pltpu.VMEM((3, 16, 8, 128), BF16),
            pltpu.VMEM((3, 16, 8, 128), BF16),
            pltpu.VMEM((3, 2, 16, half), BF16),
            pltpu.VMEM((3, 2, 16, half), BF16),
            dma((CHUNKS, len(FIRST))), dma((CHUNKS, len(FIRST))), dma((CHUNKS,)), dma((CHUNKS,)),
            dma, dma, dma((5,)), dma((7,)), dma((7,)), dma,
            dma((4,)), dma((4,)), dma((3,)), dma((3,)), dma((15,)), dma((15,)),
            dma((2,)), dma((2,)), dma((2, 3)), dma((2, 3)),
        ],
        compiler_params=pltpu.CompilerParams(
            collective_id=0, has_side_effects=True, vmem_limit_bytes=48 << 20),
        cost_estimate=pl.CostEstimate(
            flops=2 * times * times * sub, bytes_accessed=2 * times * sub, transcendentals=0),
    )(*[pltpu.with_memory_space_constraint(v, pltpu.HBM) for v in (
        snapshots, area_weight.reshape(-1, 128), eigvecs.T, eigvals.reshape(1, -1))])


def solution(mesh):
    in_specs = (P("tm", "space"), P("space"), P(), P())
    out_specs = (P(("tm", "space"), None), P("tm", "space"))
    return jax.shard_map(local, mesh=mesh, in_specs=in_specs, out_specs=out_specs, check_vma=False)
```

time: 178 us -> 166 us (0.933)
  Pallas kernels: 174 us -> 164 us
  local copies, waits for them, and re-layouts: 3.44 us -> 1.5 us
    pallas_call x1, Pallas kernels: 174 us -> 164 us  [local(): pl.pallas_call(kernel, out_shape=(jax.ShapeDtypeStruct((8, times), F32),...]
    unnamed x2, local copies, waits for them, and re-layouts: 3.44 us -> 1.5 us
where the time goes in v3:
time: 166 us
  Pallas kernels  164 us (99%)
    pallas_call x1, Pallas kernels, local(): pl.pallas_call(kernel, out_shape=(jax.ShapeDtypeStruct((8, times), F32),...  164 us

profile of v3, /device:TPU:1, one launch (start us, length us, event | category | flops | bytes accessed | tf_op | source)
XLA Modules:
  0.0 166.3 jit_solution(14348278281495282871)
XLA Ops:
  0.6 164.2 %shard_map.59 = (f32[8,1024]{1,0:T(8,128)S(1)}, bf16[8,49152]{1,0:T(8,128)(2,1)S(1)}) custom-call(bf16[128,49152]{1,0:T(8,128)(2,1)} %snap.1, f32[384,128]{1,0:T(8,128)} %bitcast.3, bf16[64,1024]{1,0:T(8,128)(2,1)} %bitcast.4, f32[1,64]{1,0:T(1,128)} %bitcast.5), custom_call_target="tpu_custom_call" | custom-call | flops 12884901888 | bytes 12582912 | tf_op jit(solution)/shard_map/pallas_call | solution.py:378
  164.8 0.6 copy.8
  165.5 0.9 copy.9

commit v4 on v3

--- a/solution.py
+++ b/solution.py
@@ -7,7 +7,7 @@
 
 MESH = pl.DeviceIdType.MESH
 CHUNKS = 12
-AHEAD = 4
+AHEAD = 6
 FIRST = (1, 2, 3, 4, 5, 7)
 LAST = 6
 BF16, F32 = jnp.bfloat16, jnp.float32
@@ -15,10 +15,12 @@
 
 def kernel(snap, area, evt_in, evals_in, gram_out, modes_out,
            buf, abuf, sbuf, asum, asum_in, means, acc, late, lrow, evt, evals, inv, area_v, mpart, msend,
-           csend, crecv, xsend, xrecv, part, ysend, yrecv,
+           csend, crecv, xsend, xrecv, part, osend, orecv, opart, isend, irecv, zsend, zrecv,
            ltc, ltc_in, lrc, lrc_in, ltx, ltx_in, lrx, lrx_in,
+           lt_part, lr_part, lty, lty_in, lry, lry_in, final,
            s_send, s_recv, a_send, a_recv, t_send, t_recv, s_local, m_send, m_recv, m_own,
-           c_send, c_recv, x_send, x_recv, y_send, y_recv, lc_send, lc_recv, lx_send, lx_recv):
+           c_send, c_recv, x_send, x_recv, o_send, o_recv, z_send, z_recv, lc_send, lc_recv, lx_send, lx_recv,
+           ly_send, ly_recv, lry_send, lry_recv):
     time_dev, cell_dev = snap.shape
     times, sub = buf.shape
     width = sub // CHUNKS
@@ -90,8 +92,6 @@
     start_chunk(0)
     for copy in local_copies:
         copy.start()
-    for k in range(1, AHEAD):
-        start_chunk(k)
 
     local_copies[0].wait()
 
@@ -101,6 +101,8 @@
     lax.fori_loop(0, CHUNKS, share, 0)
     sum_copy = rcopy(asum, asum_in, t_send, t_recv, (anti, sp))
     sum_copy.start()
+    for k in range(1, AHEAD):
+        start_chunk(k)
 
     acc[...] = jnp.zeros_like(acc)
     late[...] = jnp.zeros_like(late)
@@ -214,7 +216,7 @@
         lax.fori_loop(0, 16, pack, 0)
         core_copy(dx).start()
 
-    lax.fori_loop(0, 2, late_chunk, 0)
+    lax.fori_loop(0, 1, late_chunk, 0)
 
     for dx in order:
         core_copy(dx).wait_recv()
@@ -230,20 +232,68 @@
         if dx:
             x_copy(dx, 1).start()
 
-    lax.fori_loop(2, 9, late_chunk, 0)
+    lax.fori_loop(1, 7, late_chunk, 0)
 
     for dx in (1, 2, 3):
         x_copy(dx, -1).wait_recv()
 
-    def merge_x(g, c):
+    outer = (tm_of(4, 1), (1 - y_hi) * 8 + x * 2 + core)
+    inner = (tm_of(4, 1), sp)
+    o_copy = rcopy(osend, orecv, o_send.at[0], o_recv.at[0], outer)
+    i_copy = rcopy(isend, irecv, o_send.at[1], o_recv.at[1], inner)
+
+    def x_total(g):
         value = part[g]
         for d in range(3):
             value = value + xrecv[d, g].astype(F32)
-        part[g] = value
-        return c
-    lax.fori_loop(0, 16, merge_x, 0)
-
-    lax.fori_loop(9, CHUNKS, late_chunk, 0)
+        return value
+
+    def merge_x(t, c):
+        osend[t] = x_total(t * 2 + 1 - y_hi).astype(BF16)
+        return c
+    lax.fori_loop(0, 8, merge_x, 0)
+    o_copy.start()
+
+    def merge_own(t, c):
+        opart[t] = x_total(t * 2 + y_hi)
+        return c
+    lax.fori_loop(0, 8, merge_own, 0)
+
+    lax.fori_loop(7, 8, late_chunk, 0)
+
+    o_copy.wait_recv()
+
+    def merge_o(t, c):
+        other_t = (1 - y_lo) * 4 + t
+        isend[t] = (opart[other_t] + orecv[other_t].astype(F32)).astype(BF16)
+        return c
+    lax.fori_loop(0, 4, merge_o, 0)
+    i_copy.start()
+
+    lax.fori_loop(8, 10, late_chunk, 0)
+
+    i_copy.wait_recv()
+
+    def y_total(t):
+        own_t = y_lo * 4 + t
+        return opart[own_t] + orecv[own_t].astype(F32) + irecv[t].astype(F32)
+
+    def merge_i(t, c):
+        zsend[t] = y_total(t).astype(BF16)
+        return c
+    lax.fori_loop(0, 4, merge_i, 0)
+
+    def z_copy(dz, sign):
+        peer = tm_of(dz, sign)
+        return rcopy(zsend.at[lax.rem(peer, 4)], zrecv.at[dz - 1], z_send.at[dz - 1], z_recv.at[dz - 1],
+                     (peer, sp))
+    for dz in (1, 2, 3):
+        z_copy(dz, 1).start()
+    final_early = y_total(z)
+    final[:, :half] = final_early[:8, :]
+    final[:, half:] = final_early[8:, :]
+
+    lax.fori_loop(10, CHUNKS, late_chunk, 0)
 
     def modes_copy(j, sign):
         peer = tm_of(j, sign)
@@ -251,29 +301,28 @@
         return rcopy(msend.at[peer], modes_out.at[:, pl.ds(pl.multiple_of(col * sub, 128), sub)],
                      m_send.at[j - 1], m_recv.at[j - 1], (peer, sp))
 
+    lt_core = rcopy(ltc, ltc_in, lc_send.at[0], lc_recv.at[0], other)
+    lr_core = rcopy(lrc, lrc_in, lc_send.at[1], lc_recv.at[1], other)
+
+    def lt_x(dx, sign):
+        return rcopy(ltx.at[dx - 1], ltx_in.at[dx - 1], lx_send.at[0, dx - 1], lx_recv.at[0, dx - 1],
+                     (tm, sp_x(dx, sign)))
+
+    def lr_x(dx, sign):
+        return rcopy(lrx.at[dx - 1], lrx_in.at[dx - 1], lx_send.at[1, dx - 1], lx_recv.at[1, dx - 1],
+                     (tm, sp_x(dx, sign)))
+
+    def lt_pack(g, c):
+        for dx in range(4):
+            ltc[dx, g] = narrow(g, dx, 1 - core).astype(BF16)
+        return c
+    lax.fori_loop(0, 16, lt_pack, 0)
+    lt_core.start()
     for j in range(1, 8):
         modes_copy(j, 1).start()
     modes_own = pltpu.make_async_copy(
         msend.at[tm], modes_out.at[:, pl.ds(pl.multiple_of(tm * sub, 128), sub)], m_own)
     modes_own.start()
-
-    lt_core = rcopy(ltc, ltc_in, lc_send.at[0], lc_recv.at[0], other)
-    lr_core = rcopy(lrc, lrc_in, lc_send.at[1], lc_recv.at[1], other)
-
-    def lt_x(dx, sign):
-        return rcopy(ltx.at[dx - 1], ltx_in.at[dx - 1], lx_send.at[0, dx - 1], lx_recv.at[0, dx - 1],
-                     (tm, sp_x(dx, sign)))
-
-    def lr_x(dx, sign):
-        return rcopy(lrx.at[dx - 1], lrx_in.at[dx - 1], lx_send.at[1, dx - 1], lx_recv.at[1, dx - 1],
-                     (tm, sp_x(dx, sign)))
-
-    def lt_pack(g, c):
-        for dx in range(4):
-            ltc[dx, g] = narrow(g, dx, 1 - core).astype(BF16)
-        return c
-    lax.fori_loop(0, 16, lt_pack, 0)
-    lt_core.start()
 
     def turn(i, c):
         t = lax.rem(anti + 1 + i, 8)
@@ -285,9 +334,6 @@
         for h in range(2):
             lrc[dx, h] = unit(lrow, h, dx, 1 - core).astype(BF16)
     lr_core.start()
-
-    lane = pl.ds(pl.multiple_of(lax.rem(anti, 4) * 128, 128), 128)
-    top = pl.ds(pl.multiple_of((anti // 4) * 8, 8), 8)
 
     lt_core.wait_recv()
     for dx in order:
@@ -296,7 +342,7 @@
             if dx:
                 ltx[dx - 1, g] = value.astype(BF16)
             else:
-                part[g, top, lane] += value
+                lt_part[g] = value
             return c
         lax.fori_loop(0, 16, lt_merge, 0)
         if dx:
@@ -308,42 +354,59 @@
             if dx:
                 lrx[dx - 1, h] = value.astype(BF16)
             else:
-                part[anti * 2 + h] += value
+                lr_part[h] = value
         if dx:
             lr_x(dx, 1).start()
     for dx in (1, 2, 3):
         lt_x(dx, -1).wait_recv()
 
     def lt_sum(g, c):
-        value = part[g, top, lane]
+        value = lt_part[g]
         for d in range(3):
             value = value + ltx_in[d, g].astype(F32)
-        part[g, top, lane] = value
+        lt_part[g] = value
+        lty[g] = value.astype(BF16)
         return c
     lax.fori_loop(0, 16, lt_sum, 0)
+
+    def lt_y(j, sign):
+        t, h = yz_of(j, sign)
+        return rcopy(lty.at[t * 2 + h], lty_in.at[j - 1], ly_send.at[j - 1], ly_recv.at[j - 1],
+                     (t, h * 8 + x * 2 + core))
+
+    for j in range(1, 16):
+        lt_y(j, 1).start()
+
     for dx in (1, 2, 3):
         lr_x(dx, -1).wait_recv()
     for h in range(2):
-        value = part[anti * 2 + h]
+        value = lr_part[h]
         for d in range(3):
             value = value + lrx_in[d, h].astype(F32)
-        part[anti * 2 + h] = value
-
-    def y_copy(j, sign):
-        t, h = yz_of(j, sign)
-        return rcopy(ysend.at[t * 2 + h], yrecv.at[j - 1], y_send.at[j - 1], y_recv.at[j - 1],
+        lry[h] = value.astype(BF16)
+
+    def lr_y(i, sign):
+        t, h = yz_of(LAST + 8 * i, sign)
+        return rcopy(lry.at[h], lry_in.at[i], lry_send.at[i], lry_recv.at[i],
                      (t, h * 8 + x * 2 + core))
 
-    def y_pack(g, c):
-        ysend[g] = part[g].astype(BF16)
-        return c
-    lax.fori_loop(0, 16, y_pack, 0)
+    for i in range(2):
+        lr_y(i, 1).start()
+
+    for dz in (1, 2, 3):
+        z_copy(dz, -1).wait_recv()
+        value = zrecv[dz - 1].astype(F32)
+        final[:, :half] += value[:8, :]
+        final[:, half:] += value[8:, :]
+    final[:, block_rows(anti)] += lt_part[tm * 2 + y_hi]
     for j in range(1, 16):
-        y_copy(j, 1).start()
-    total = part[tm * 2 + y_hi]
-    for j in range(1, 16):
-        y_copy(j, -1).wait_recv()
-        total = total + yrecv[j - 1].astype(F32)
+        lt_y(j, -1).wait_recv()
+        facing = (j // 4 + 1) % 2 * 4 + (j + 2) % 4
+        final[:, block_rows(tm_of(facing, -1))] += lty_in[j - 1].astype(F32)
+    total = jnp.concatenate([final[:, :half], final[:, half:]], axis=0)
+    for i in range(2):
+        lr_y(i, -1).wait_recv()
+        total = total + lry_in[i].astype(F32)
     total = total / cells
     gram_out[:, :half] = total[:8, :]
     gram_out[:, half:] = total[8:, :]
@@ -357,12 +420,17 @@
         core_copy(dx).wait_send()
     lt_core.wait_send()
     lr_core.wait_send()
+    o_copy.wait_send()
+    i_copy.wait_send()
     for dx in (1, 2, 3):
         x_copy(dx, 1).wait_send()
+        z_copy(dx, 1).wait_send()
         lt_x(dx, 1).wait_send()
         lr_x(dx, 1).wait_send()
     for j in range(1, 16):
-        y_copy(j, 1).wait_send()
+        lt_y(j, 1).wait_send()
+    for i in range(2):
+        lr_y(i, 1).wait_send()
 
 
 def local(snapshots, area_weight, eigvecs, eigvals):
@@ -401,8 +469,13 @@
             pltpu.VMEM((3, 16, 16, half), BF16),
             pltpu.VMEM((3, 16, 16, half), BF16),
             pltpu.VMEM((16, 16, half), F32),
-            pltpu.VMEM((16, 16, half), BF16),
-            pltpu.VMEM((15, 16, half), BF16),
+            pltpu.VMEM((8, 16, half), BF16),
+            pltpu.VMEM((8, 16, half), BF16),
+            pltpu.VMEM((8, 16, half), F32),
+            pltpu.VMEM((4, 16, half), BF16),
+            pltpu.VMEM((4, 16, half), BF16),
+            pltpu.VMEM((4, 16, half), BF16),
+            pltpu.VMEM((3, 16, half), BF16),
             pltpu.VMEM((4, 16, 8, 128), BF16),
             pltpu.VMEM((4, 16, 8, 128), BF16),
             pltpu.VMEM((4, 2, 16, half), BF16),
@@ -411,10 +484,18 @@
             pltpu.VMEM((3, 16, 8, 128), BF16),
             pltpu.VMEM((3, 2, 16, half), BF16),
             pltpu.VMEM((3, 2, 16, half), BF16),
+            pltpu.VMEM((16, 8, 128), F32),
+            pltpu.VMEM((2, 16, half), F32),
+            pltpu.VMEM((16, 8, 128), BF16),
+            pltpu.VMEM((15, 8, 128), BF16),
+            pltpu.VMEM((2, 16, half), BF16),
+            pltpu.VMEM((2, 16, half), BF16),
+            pltpu.VMEM((8, times), F32),
             dma((CHUNKS, len(FIRST))), dma((CHUNKS, len(FIRST))), dma((CHUNKS,)), dma((CHUNKS,)),
             dma, dma, dma((5,)), dma((7,)), dma((7,)), dma,
-            dma((4,)), dma((4,)), dma((3,)), dma((3,)), dma((15,)), dma((15,)),
+            dma((4,)), dma((4,)), dma((3,)), dma((3,)), dma((2,)), dma((2,)), dma((3,)), dma((3,)),
             dma((2,)), dma((2,)), dma((2, 3)), dma((2, 3)),
+            dma((15,)), dma((15,)), dma((2,)), dma((2,)),
         ],
         compiler_params=pltpu.CompilerParams(
             collective_id=0, has_side_effects=True, vmem_limit_bytes=48 << 20),

time: 166 us -> 163 us (0.982)
  Pallas kernels: 164 us -> 161 us
    pallas_call x1, Pallas kernels: 164 us -> 161 us  [local(): pl.pallas_call(kernel, out_shape=(jax.ShapeDtypeStruct((8, times), F32),...]
where the time goes in v4:
time: 163 us
  Pallas kernels  161 us (99%)
    pallas_call x1, Pallas kernels, local(): pl.pallas_call(kernel, out_shape=(jax.ShapeDtypeStruct((8, times), F32),...  161 us

profile of v4, /device:TPU:1, one launch (start us, length us, event | category | flops | bytes accessed | tf_op | source)
XLA Modules:
  0.0 163.3 jit_solution(12624647459274587786)
XLA Ops:
  0.6 161.1 %shard_map.59 = (f32[8,1024]{1,0:T(8,128)S(1)}, bf16[8,49152]{1,0:T(8,128)(2,1)S(1)}) custom-call(bf16[128,49152]{1,0:T(8,128)(2,1)} %snap.1, f32[384,128]{1,0:T(8,128)} %bitcast.3, bf16[64,1024]{1,0:T(8,128)(2,1)} %bitcast.4, f32[1,64]{1,0:T(1,128)} %bitcast.5), custom_call_target="tpu_custom_call" | custom-call | flops 12884901888 | bytes 12582912 | tf_op jit(solution)/shard_map/pallas_call | solution.py:446
  161.8 0.6 copy.8
  162.4 0.9 copy.9

commit v5 on v4

--- a/solution.py
+++ b/solution.py
@@ -433,6 +433,15 @@
         lr_y(i, 1).wait_send()
 
 
+def hand_over(gram, modes, gram_out, modes_out, sems):
+    copies = [pltpu.make_async_copy(gram, gram_out, sems.at[0]),
+              pltpu.make_async_copy(modes, modes_out, sems.at[1])]
+    for copy in copies:
+        copy.start()
+    for copy in copies:
+        copy.wait()
+
+
 def local(snapshots, area_weight, eigvecs, eigvals):
     tm_count = lax.axis_size("tm")
     time_dev, cell_dev = snapshots.shape
@@ -443,7 +452,7 @@
     vmem = pl.BlockSpec(memory_space=pltpu.VMEM)
     hbm = pl.BlockSpec(memory_space=pltpu.HBM)
     dma = pltpu.SemaphoreType.DMA
-    return pl.pallas_call(
+    results = pl.pallas_call(
         kernel,
         out_shape=(jax.ShapeDtypeStruct((8, times), F32), jax.ShapeDtypeStruct((8, cell_dev), BF16)),
         in_specs=[hbm] * 4,
@@ -503,6 +512,14 @@
             flops=2 * times * times * sub, bytes_accessed=2 * times * sub, transcendentals=0),
     )(*[pltpu.with_memory_space_constraint(v, pltpu.HBM) for v in (
         snapshots, area_weight.reshape(-1, 128), eigvecs.T, eigvals.reshape(1, -1))])
+    return pl.pallas_call(
+        hand_over,
+        out_shape=[jax.ShapeDtypeStruct(v.shape, v.dtype) for v in results],
+        in_specs=[vmem] * 2,
+        out_specs=[pl.BlockSpec(memory_space=pltpu.HBM)] * 2,
+        scratch_shapes=[dma((2,))],
+        compiler_params=pltpu.CompilerParams(vmem_limit_bytes=2 << 20),
+    )(*results)
 
 
 def solution(mesh):

time: 163 us -> 163 us (level)
  no operation moved by 1% of the time
where the time goes in v5:
time: 163 us
  Pallas kernels  162 us (99%)
    pallas_call x1, Pallas kernels, local(): pl.pallas_call(kernel, out_shape=(jax.ShapeDtypeStruct((8, times), F32),...  161 us

profile of v5, /device:TPU:1, one launch (start us, length us, event | category | flops | bytes accessed | tf_op | source)
XLA Modules:
  0.0 162.7 jit_solution(11211921175493169442)
XLA Ops:
  0.6 161.1 %shard_map.59 = (f32[8,1024]{1,0:T(8,128)S(1)}, bf16[8,49152]{1,0:T(8,128)(2,1)S(1)}) custom-call(bf16[128,49152]{1,0:T(8,128)(2,1)} %snap.1, f32[384,128]{1,0:T(8,128)} %bitcast.3, bf16[64,1024]{1,0:T(8,128)(2,1)} %bitcast.4, f32[1,64]{1,0:T(1,128)} %bitcast.5), custom_call_target="tpu_custom_call" | custom-call | flops 12884901888 | bytes 12582912 | tf_op jit(solution)/shard_map/pallas_call | solution.py:455
  161.8 0.9 shard_map.60

commit v6 on v5

--- a/solution.py
+++ b/solution.py
@@ -270,30 +270,7 @@
     lax.fori_loop(0, 4, merge_o, 0)
     i_copy.start()
 
-    lax.fori_loop(8, 10, late_chunk, 0)
-
-    i_copy.wait_recv()
-
-    def y_total(t):
-        own_t = y_lo * 4 + t
-        return opart[own_t] + orecv[own_t].astype(F32) + irecv[t].astype(F32)
-
-    def merge_i(t, c):
-        zsend[t] = y_total(t).astype(BF16)
-        return c
-    lax.fori_loop(0, 4, merge_i, 0)
-
-    def z_copy(dz, sign):
-        peer = tm_of(dz, sign)
-        return rcopy(zsend.at[lax.rem(peer, 4)], zrecv.at[dz - 1], z_send.at[dz - 1], z_recv.at[dz - 1],
-                     (peer, sp))
-    for dz in (1, 2, 3):
-        z_copy(dz, 1).start()
-    final_early = y_total(z)
-    final[:, :half] = final_early[:8, :]
-    final[:, half:] = final_early[8:, :]
-
-    lax.fori_loop(10, CHUNKS, late_chunk, 0)
+    lax.fori_loop(8, CHUNKS, late_chunk, 0)
 
     def modes_copy(j, sign):
         peer = tm_of(j, sign)
@@ -357,6 +334,27 @@
                 lr_part[h] = value
         if dx:
             lr_x(dx, 1).start()
+    i_copy.wait_recv()
+
+    def y_total(t):
+        own_t = y_lo * 4 + t
+        return opart[own_t] + orecv[own_t].astype(F32) + irecv[t].astype(F32)
+
+    def merge_i(t, c):
+        zsend[t] = y_total(t).astype(BF16)
+        return c
+    lax.fori_loop(0, 4, merge_i, 0)
+
+    def z_copy(dz, sign):
+        peer = tm_of(dz, sign)
+        return rcopy(zsend.at[lax.rem(peer, 4)], zrecv.at[dz - 1], z_send.at[dz - 1], z_recv.at[dz - 1],
+                     (peer, sp))
+    for dz in (1, 2, 3):
+        z_copy(dz, 1).start()
+    final_early = y_total(z)
+    final[:, :half] = final_early[:8, :]
+    final[:, half:] = final_early[8:, :]
+
     for dx in (1, 2, 3):
         lt_x(dx, -1).wait_recv()
 
@@ -371,7 +369,7 @@
 
     def lt_y(j, sign):
         t, h = yz_of(j, sign)
-        return rcopy(lty.at[t * 2 + h], lty_in.at[j - 1], ly_send.at[j - 1], ly_recv.at[j - 1],
+        return rcopy(lty.at[t * 2 + h], lty_in.at[j - 1], ly_send, ly_recv,
                      (t, h * 8 + x * 2 + core))
 
     for j in range(1, 16):
@@ -399,8 +397,9 @@
         final[:, :half] += value[:8, :]
         final[:, half:] += value[8:, :]
     final[:, block_rows(anti)] += lt_part[tm * 2 + y_hi]
+    all_y = rcopy(lty.at[pl.ds(0, 15)], lty_in, ly_send, ly_recv, other)
+    all_y.wait_recv()
     for j in range(1, 16):
-        lt_y(j, -1).wait_recv()
         facing = (j // 4 + 1) % 2 * 4 + (j + 2) % 4
         final[:, block_rows(tm_of(facing, -1))] += lty_in[j - 1].astype(F32)
     total = jnp.concatenate([final[:, :half], final[:, half:]], axis=0)
@@ -427,8 +426,7 @@
         z_copy(dx, 1).wait_send()
         lt_x(dx, 1).wait_send()
         lr_x(dx, 1).wait_send()
-    for j in range(1, 16):
-        lt_y(j, 1).wait_send()
+    all_y.wait_send()
     for i in range(2):
         lr_y(i, 1).wait_send()
 
@@ -504,7 +502,7 @@
             dma, dma, dma((5,)), dma((7,)), dma((7,)), dma,
             dma((4,)), dma((4,)), dma((3,)), dma((3,)), dma((2,)), dma((2,)), dma((3,)), dma((3,)),
             dma((2,)), dma((2,)), dma((2, 3)), dma((2, 3)),
-            dma((15,)), dma((15,)), dma((2,)), dma((2,)),
+            dma, dma, dma((2,)), dma((2,)),
         ],
         compiler_params=pltpu.CompilerParams(
             collective_id=0, has_side_effects=True, vmem_limit_bytes=48 << 20),

time: 163 us -> 163 us (level)
  no operation moved by 1% of the time
where the time goes in v6:
time: 163 us; the launch traced here: 162 us
  Pallas kernels  162 us (99%)
    pallas_call x1, Pallas kernels, local(): pl.pallas_call(kernel, out_shape=(jax.ShapeDtypeStruct((8, times), F32),...  161 us

profile of v6, /device:TPU:1, one launch (start us, length us, event | category | flops | bytes accessed | tf_op | source)
XLA Modules:
  0.0 162.4 jit_solution(2007999464930870667)
XLA Ops:
  0.6 160.9 %shard_map.59 = (f32[8,1024]{1,0:T(8,128)S(1)}, bf16[8,49152]{1,0:T(8,128)(2,1)S(1)}) custom-call(bf16[128,49152]{1,0:T(8,128)(2,1)} %snap.1, f32[384,128]{1,0:T(8,128)} %bitcast.3, bf16[64,1024]{1,0:T(8,128)(2,1)} %bitcast.4, f32[1,64]{1,0:T(1,128)} %bitcast.5), custom_call_target="tpu_custom_call" | custom-call | flops 12884901888 | bytes 12582912 | tf_op jit(solution)/shard_map/pallas_call | solution.py:453
  161.5 0.9 shard_map.60
